TPU v7x, 128 devices: a whole 4x4x4 slice. The times are simulated.
128 devices in a mesh: row: 8 (over y, core), col: 16 (over x, z).
Axes of the slice: x: 4, y: 4, z: 4, core: 2. Of those that a mesh axis runs over, the one named last changes fastest.
Arguments:
- features: bfloat16 [32768, 128], P(('row', 'col')), may hold values from -6 to 6
- tile_values: bfloat16 [8, 16, 512, 128, 128], P('row', 'col'), may hold values from -0.03125 to 0.03125
- tile_coords: int32 [8, 16, 2, 512], P('row', 'col'), may hold values from 0 to 31, as said below
- tile_count: int32 [8, 16], P('row', 'col'), may hold values from 128 to 512, as said below
- weight: bfloat16 [128, 256], replicated, may hold values from -0.5 to 0.5
- bias: float32 [256], replicated, may hold values from -3 to 3
- cotangent: bfloat16 [32768, 256], P(('row', 'col')), may hold values from -6 to 6
Outputs:
- layer_out: bfloat16 [32768, 256], P(('row', 'col'))
- weight_grad: float32 [128, 256], replicated
- bias_grad: float32 [256], replicated
- feature_grad: float32 [32768, 128], P(('row', 'col'))
Inputs may be any that keep to these rules, and one draw needn't show every extreme that they name: `tile_coords`: each device's tile row entries lie below 32 and tile column entries below 16, in every slot; some device has a tile row 31. `tile_count`: some device has all 512 slots live.
All inputs are finite; a program needn't handle non-finite values.
Results may differ from a plain program's by a relative error of at most 0.007.
Values may be sent and summed in bfloat16 or wider, within the bound.
A program may use at most 192 MiB of HBM per device.

v0:
```python
import math

import jax
import jax.numpy as jnp
from jax import lax
from jax.sharding import PartitionSpec as P


def tile_terms(values, in_index, source, transposed):
    feat_width = source.shape[1]
    block_side = values.shape[1]
    block_total = source.shape[0] // block_side
    flat_blocks = source.reshape(block_total, block_side * feat_width)
    selector = (in_index[:, None] == jnp.arange(block_total, dtype=jnp.int32)[None, :]).astype(
        jnp.bfloat16
    )
    picked = jnp.dot(selector, flat_blocks, preferred_element_type=jnp.float32).astype(jnp.bfloat16)
    picked = picked.reshape(values.shape[0], block_side, feat_width)
    if transposed:
        return jnp.einsum("tji,tjf->tif", values, picked, preferred_element_type=jnp.float32)
    return jnp.einsum("tij,tjf->tif", values, picked, preferred_element_type=jnp.float32)


def place_terms(products, out_index, tile_total, first_block, segments):
    tile_slots = products.shape[0]
    alive_mask = jnp.arange(tile_slots, dtype=jnp.int32) < tile_total
    shifted = out_index - first_block
    seg_ids = jnp.arange(segments, dtype=jnp.int32)
    placer = ((shifted[None, :] == seg_ids[:, None]) & alive_mask[None, :]).astype(jnp.float32)
    flat_terms = products.reshape(tile_slots, products.shape[1] * products.shape[2])
    summed = jnp.dot(
        placer, flat_terms, precision=lax.Precision.HIGHEST, preferred_element_type=jnp.float32
    )
    return summed.reshape(segments * products.shape[1], products.shape[2])


def local(features, tile_values, tile_coords, tile_count, weight, bias, cotangent):
    values = tile_values[0, 0]
    coords = tile_coords[0, 0]
    tile_total = tile_count[0, 0]
    own_rows = features.shape[0]
    block_side = values.shape[1]
    row_blocks = lax.axis_size("col") * own_rows // block_side
    col_blocks = lax.axis_size("row") * own_rows // block_side
    column_feats = lax.all_gather(features, "row", axis=0, tiled=True)
    products = tile_terms(values, coords[1], column_feats, False)
    partial_value = place_terms(products, coords[0], tile_total, 0, row_blocks)
    aggregated = lax.psum_scatter(partial_value, "col", scatter_dimension=0, tiled=True)
    agg_bf = aggregated.astype(jnp.bfloat16)
    pre = jnp.dot(agg_bf, weight, preferred_element_type=jnp.float32) + bias
    sigma = jax.nn.sigmoid(pre)
    layer_out = (pre * sigma).astype(jnp.bfloat16)
    slope_grad = (cotangent.astype(jnp.float32) * sigma * (1.0 + pre * (1.0 - sigma))).astype(
        jnp.bfloat16
    )
    local_weight = lax.dot_general(
        agg_bf, slope_grad, (((0,), (0,)), ((), ())), preferred_element_type=jnp.float32
    )
    local_bias = jnp.sum(slope_grad.astype(jnp.float32), axis=0)
    scale_factor = 1.0 / math.sqrt(own_rows * lax.axis_size("row") * lax.axis_size("col"))
    summed_weight, summed_bias = lax.psum((local_weight, local_bias), ("row", "col"))
    weight_grad = summed_weight * scale_factor
    bias_grad = summed_bias * scale_factor
    vertex_grad = lax.dot_general(
        slope_grad, weight, (((1,), (1,)), ((), ())), preferred_element_type=jnp.float32
    ).astype(jnp.bfloat16)
    group_grads = lax.all_gather(vertex_grad, "col", axis=0, tiled=True)
    back_products = tile_terms(values, coords[0], group_grads, True)
    back_partial = place_terms(back_products, coords[1], tile_total, 0, col_blocks)
    feature_grad = lax.psum_scatter(back_partial, "row", scatter_dimension=0, tiled=True)
    return (layer_out, weight_grad, bias_grad, feature_grad)


def solution(mesh):
    placed = (
        P(("row", "col"), None),
        P("row", "col", None, None, None),
        P("row", "col", None, None),
        P("row", "col"),
        P(),
        P(),
        P(("row", "col"), None),
    )
    return jax.shard_map(
        local,
        mesh=mesh,
        in_specs=placed,
        out_specs=(P(("row", "col"), None), P(), P(), P(("row", "col"), None)),
        check_vma=False,
    )
```

profile of v0, /device:TPU:1, one launch (start us, length us, event | category | flops | bytes accessed | tf_op | source)
XLA Modules:
  0.0 421.2 jit_solution(6334156852055594432)
XLA Ops:
  7.2 0.0 reduce-scatter.3.cloned.1.call-start
  7.9 0.8 fusion.27
  8.7 15.2 %all_gather.6 = bf16[2048,128]{1,0:T(8,128)(2,1)S(1)} all-gather(bf16[256,128]{1,0:T(8,128)(2,1)} %param.7), channel_id=1, replica_groups=mesh['row'=8,'col'=16] {'row'}, dimensions={0}, use_global_device_ids=true | all-gather | bytes 589824 | tf_op jit(solution)/shard_map/all_gather | solution.py:45
  23.8 0.2 reshape.45
  24.0 4.8 %fusion.11 = bf16[64,8,128,128]{3,1,2,0:T(8,128)(2,1)S(1)} fusion(bf16[16,16384]{1,0:T(8,128)(2,1)S(1)} %reshape.45, s32[512]{0:T(512)S(1)} %bitcast.39), kind=kOutput, calls=%fused_computation.9 | convolution fusion | flops 276832256 | bytes 17303552 | tf_op jit(solution)/shard_map/dot_general | solution.py:17
  28.9 8.3 %copy.19 = bf16[64,8,128,128]{3,2,1,0:T(8,128)(2,1)} copy(bf16[64,8,128,128]{3,1,2,0:T(8,128)(2,1)S(1)} %fusion.11) | data formatting | bytes 33554432
  37.2 25.2 %fusion.4 = f32[512,128,128]{1,2,0:T(8,128)} fusion(bf16[512,128,128]{2,1,0:T(8,128)(2,1)} %bitcast.37, bf16[1,1,512,128,128]{4,3,2,1,0:T(8,128)(2,1)} %param.8), kind=kOutput, calls=%fused_computation.6 | convolution fusion | flops 2147483648 | bytes 67108864 | tf_op jit(solution)/shard_map/tij,tjf->tif/dot_general | solution.py:21
  62.4 34.8 %copy.14 = f32[512,128,128]{0,2,1:T(8,128)} copy(f32[512,128,128]{1,2,0:T(8,128)} %fusion.4) | data formatting | bytes 67108864 | tf_op jit(solution)/shard_map/tij,tjf->tif/dot_general | solution.py:21
  97.2 20.5 %fusion.15 = f32[32,16384]{1,0:T(8,128)S(1)} fusion(f32[512,16384]{0,1:T(8,128)} %bitcast.36, s32[512]{0:T(512)S(1)} %bitcast.41, pred[512]{0:T(512)(128)(4,1)S(1)} %iota_compare_fusion.6), kind=kOutput, calls=%fused_computation.23 | convolution fusion | flops 3221258240 | bytes 35654144 | tf_op jit(solution)/shard_map/dot_general | solution.py:31
  117.7 1.5 reshape.48
  119.2 0.0 reduce-scatter.3.cloned.1.call-update
  119.2 0.0 all-gather.2.cloned.1.call-start
  119.3 74.2 %reduce-scatter.3.cloned.1.call-done = f32[256,128]{1,0:T(8,128)} async-done(((f32[4096,128]{1,0:T(8,128)}), f32[256,128]{1,0:T(8,128)}) %reduce-scatter.3.cloned.1.call-update) | async-done | bytes 131088 | tf_op jit(solution)/shard_map/reduce_scatter | solution.py:48
  193.5 1.8 convert_reduce_fusion
  195.3 0.8 convolution_convert_fusion.2
  196.2 0.0 all-reduce.2.cloned.1.call-start
  196.2 1.8 fusion.17
  198.0 0.0 all-reduce.2.cloned.1.call-update
  198.0 0.2 reduce-scatter.5.cloned.1.call-start
  198.2 40.4 %all-gather.2.cloned.1.call-done = bf16[4096,128]{1,0:T(8,128)(2,1)} async-done(((bf16[256,128]{1,0:T(8,128)(2,1)}), bf16[4096,128]{1,0:T(8,128)(2,1)}) %all-gather.2.cloned.1.call-update) | async-done | bytes 1048592 | tf_op jit(solution)/shard_map/all_gather | solution.py:67
  238.6 1.5 reshape.49
  240.1 4.8 %fusion.10 = bf16[64,8,128,128]{3,1,2,0:T(8,128)(2,1)S(1)} fusion(bf16[32,16384]{1,0:T(8,128)(2,1)S(1)} %reshape.49, s32[512]{0:T(512)S(1)} %bitcast.42), kind=kOutput, calls=%fused_computation.8 | convolution fusion | flops 545275904 | bytes 17827840 | tf_op jit(solution)/shard_map/dot_general | solution.py:17
  244.9 8.3 %copy.20 = bf16[64,8,128,128]{3,2,1,0:T(8,128)(2,1)} copy(bf16[64,8,128,128]{3,1,2,0:T(8,128)(2,1)S(1)} %fusion.10) | data formatting | bytes 33554432
  253.2 24.7 %fusion.7 = f32[512,128,128]{1,2,0:T(8,128)} fusion(bf16[512,128,128]{2,1,0:T(8,128)(2,1)} %bitcast.38, bf16[1,1,512,128,128]{4,3,2,1,0:T(8,128)(2,1)} %param.8), kind=kOutput, calls=%fused_computation.7 | convolution fusion | flops 2147483648 | bytes 67108864 | tf_op jit(solution)/shard_map/tji,tjf->tif/dot_general | solution.py:20
  277.9 34.8 %copy.16 = f32[512,128,128]{0,2,1:T(8,128)} copy(f32[512,128,128]{1,2,0:T(8,128)} %fusion.7) | data formatting | bytes 67108864 | tf_op jit(solution)/shard_map/tji,tjf->tif/dot_general | solution.py:20
  312.7 18.7 %fusion.22 = f32[16,16384]{1,0:T(8,128)S(1)} fusion(f32[512,16384]{0,1:T(8,128)} %bitcast.35, s32[512]{0:T(512)S(1)} %bitcast.40, pred[512]{0:T(512)(128)(4,1)S(1)} %iota_compare_fusion.6), kind=kOutput, calls=%fused_computation.30 | convolution fusion | flops 1610629120 | bytes 34605568 | tf_op jit(solution)/shard_map/dot_general | solution.py:31
  331.4 1.1 reshape.52
  332.6 0.0 reduce-scatter.5.cloned.1.call-update
  332.6 65.7 %psum.15 = f32[256]{0:T(256)S(1)} all-reduce(f32[256]{0:T(256)S(1)} %get-tuple-element.4), channel_id=1, replica_groups=mesh['row'=8,'col'=16] {'row','col'}, use_global_device_ids=true, to_apply=%region_3.0 | all-reduce | flops 256 | bytes 2048 | tf_op jit(solution)/shard_map/psum | solution.py:61
  398.2 0.6 broadcast_multiply_fusion.1
  398.8 1.6 broadcast_multiply_fusion
  400.4 14.3 %reduce-scatter.5.cloned.1.call-done = f32[256,128]{1,0:T(8,128)} async-done(((f32[2048,128]{1,0:T(8,128)}), f32[256,128]{1,0:T(8,128)}) %reduce-scatter.5.cloned.1.call-update) | async-done | bytes 131088 | tf_op jit(solution)/shard_map/reduce_scatter | solution.py:70
  (9 shorter events, 0.0 us)
Async XLA Ops:
  7.2 186.3 %copy-start = (bf16[128,256]{1,0:T(8,128)(2,1)S(1)}, bf16[128,256]{1,0:T(8,128)(2,1)}, u32[]{:S(2)}) copy-start(bf16[128,256]{1,0:T(8,128)(2,1)} %param.11) | copy-start | bytes 196612
  7.2 186.3 %reduce-scatter.3.cloned.1.call-start = ((), (), s32[]{:S(2)}) async-start(), calls=%async_computation.2 | async-start | bytes 2228224 | tf_op jit(solution)/shard_map/reduce_scatter | solution.py:48
  97.2 96.3 %copy-start.1 = (bf16[256,256]{1,0:T(8,128)(2,1)S(1)}, bf16[256,256]{1,0:T(8,128)(2,1)}, u32[]{:S(2)}) copy-start(bf16[256,256]{1,0:T(8,128)(2,1)} %param.13) | copy-start | bytes 393220
  97.2 96.3 %copy-start.2 = (f32[256]{0:T(256)S(1)}, f32[256]{0:T(256)}, u32[]{:S(2)}) copy-start(f32[256]{0:T(256)} %param.12) | copy-start | bytes 3076
  119.2 119.4 %all-gather.2.cloned.1.call-start = ((), (), s32[]{:S(2)}) async-start(), calls=%async_computation.4 | async-start | bytes 1114112 | tf_op jit(solution)/shard_map/all_gather | solution.py:67
  196.2 202.6 %all-reduce.2.cloned.1.call-start = ((), (), s32[]{:S(2)}) async-start(), calls=%async_computation.3 | async-start | bytes 262144 | tf_op jit(solution)/shard_map/psum | solution.py:61
  198.0 216.7 %reduce-scatter.5.cloned.1.call-start = ((), (), s32[]{:S(2)}) async-start(), calls=%async_computation.5 | async-start | bytes 1179648 | tf_op jit(solution)/shard_map/reduce_scatter | solution.py:70
Sparse Core Ops, SparseCore 0:
  119.4 74.0 reduce-scatter.2
  196.4 42.1 all-gather.1
  244.6 140.7 all-reduce.1
  388.2 26.4 reduce-scatter.4
where the time goes:
time: 425 us; the launch traced here: 421 us
  waiting for transfers between devices  129 us (30%)
  matrix products  103 us (24%)
  local copies, waits for them, and re-layouts  91.4 us (22%)
  blocking collectives  80.8 us (19%)
  between operations  14.5 us (3%)
    reduce_scatter x1, waiting for transfers between devices, local(): lax.psum_scatter(partial_value, 'col', scatter_dimension=0, tiled=True)  74.2 us
    psum x1, blocking collectives, local(): lax.psum((local_weight, local_bias), ('row', 'col'))  65.7 us
    all_gather x1, waiting for transfers between devices, local(): group_grads = lax.all_gather(vertex_grad, 'col', axis=0, tiled=True)  40.4 us
    dot_general x2, matrix products, place_terms(): jnp.dot(placer, flat_terms, precision=lax.Precision.HIGHEST, preferred_el...  39.3 us
    dot_general x1, local copies, waits for them, and re-layouts, tile_terms(): jnp.einsum('tji,tjf->tif', values, picked, preferred_element_type=jnp.flo...  34.8 us
    dot_general x1, local copies, waits for them, and re-layouts, tile_terms(): jnp.einsum('tij,tjf->tif', values, picked, preferred_element_type=jnp.flo...  34.8 us
    dot_general x1, matrix products, tile_terms(): jnp.einsum('tij,tjf->tif', values, picked, preferred_element_type=jnp.flo...  25.2 us
    dot_general x1, matrix products, tile_terms(): jnp.einsum('tji,tjf->tif', values, picked, preferred_element_type=jnp.flo...  24.7 us
  transfers between devices with their start and end apart: 4, of which 3 were waited for; matrix products, arithmetic and copies ran while one was open for 23% of the time, Pallas kernels for 0%

commit v1 on v0

v1 whole, which is shorter than its diff:
```python
import functools
import math

import jax
import jax.numpy as jnp
from jax import lax
from jax.experimental import pallas as pl
from jax.experimental.pallas import tpu as pltpu
from jax.sharding import PartitionSpec as P

f32, bf16, i32 = jnp.float32, jnp.bfloat16, jnp.int32
MESH = pl.DeviceIdType.MESH
BLK = 128
LOADS = 8


def kernel(
    feats_hbm, tiles_hbm, coords_hbm, count_ref, weight_hbm, bias_ref, cot_hbm,
    out_ref, wgrad_ref, bgrad_ref, fgrad_ref,
    raw, slots, xg, coords, weight, cot, meta_v, meta,
    part, recv_a, recv_b, sum_a, sum_b, recv_a2, recv_b2,
    grads, back, rs1_out, rs1_in, rs2_out, rs2_in,
    w1, w2, w3, w4, w5, w6,
    load_sem, send_sem, recv_sem,
):
    tiles = raw.shape[0]
    row, col = lax.axis_index("row"), lax.axis_index("col")
    y, core = lax.div(row, 2), lax.rem(row, 2)
    x, z = lax.div(col, 4), lax.rem(col, 4)

    def device(dy=0, dcore=0, dx=0, dz=0):
        return (
            lax.rem(y + dy, 4) * 2 + lax.rem(core + dcore, 2),
            lax.rem(x + dx, 4) * 4 + lax.rem(z + dz, 4),
        )

    counter = [0]

    def remote(src, dst, sem, **where):
        return pltpu.make_async_remote_copy(
            src_ref=src,
            dst_ref=dst,
            send_sem=send_sem.at[sem],
            recv_sem=recv_sem.at[sem],
            device_id=device(**where),
            device_id_type=MESH,
        )

    def take(count):
        first = counter[0]
        counter[0] += count
        return first

    sent = []

    def send(*args, **where):
        copy = remote(*args, **where)
        copy.start()
        sent.append(copy)
        return copy

    barrier = pltpu.get_barrier_semaphore()
    peers = [device(dcore=1)]
    for d in (1, 2, 3):
        peers += [device(dy=d), device(dx=d), device(dz=d)]
    for peer in peers:
        pl.semaphore_signal(barrier, inc=1, device_id=peer, device_id_type=MESH)

    def load(src, dst, sem):
        copy = pltpu.make_async_copy(src, dst, load_sem.at[sem])
        copy.start()
        return copy

    coords_load = load(coords_hbm.at[0, 0], coords, 0)
    feats_load = load(feats_hbm, xg.at[row], 1)
    step = tiles // LOADS
    tile_loads = [
        load(
            tiles_hbm.at[0, 0, pl.ds(n * step, step)],
            raw.at[pl.ds(n * step, step)],
            4 + n,
        )
        for n in range(LOADS)
    ]
    weight_load = load(weight_hbm, weight, 2)
    cot_load = load(cot_hbm, cot, 3)

    slots[tiles] = jnp.zeros((BLK, BLK), bf16)
    coords_load.wait()
    lanes = lax.broadcasted_iota(i32, (1, tiles), 1)
    live = lanes < count_ref[0, 0]
    pos = jnp.where(live, coords[0:1, :] * 16 + coords[1:2, :], tiles)
    key = pos * tiles + lanes

    def down(v):
        return jnp.transpose(jnp.broadcast_to(v, (BLK, tiles)))

    def count(mask):
        return jnp.sum(jnp.where(mask, 1, 0), axis=0, keepdims=True)

    pos_down, key_down = down(pos), down(key)
    rank, first = [], []
    for n in range(tiles // BLK):
        cut = slice(n * BLK, (n + 1) * BLK)
        before = key_down < key[:, cut]
        rank.append(count(before))
        first.append(count(before & (pos_down == pos[:, cut])))
    rank = jnp.concatenate(rank, axis=1)
    first = jnp.concatenate(first, axis=1)
    code = lanes * 2 + jnp.where(first == 0, 1, 0)
    rank_down, code_down = down(rank), down(code)
    for n in range(tiles // BLK):
        cut = slice(n * BLK, (n + 1) * BLK)
        at = lanes[:, cut]
        meta_v[0:1, cut] = jnp.sum(jnp.where(rank_down == at, code_down, 0), axis=0, keepdims=True)
        upto, here = count(pos_down <= at), count(pos_down == at)
        meta_v[1:2, cut] = jnp.where(here == 0, tiles, upto - 1)
    meta_load = load(meta_v, meta, 0)

    pl.semaphore_wait(barrier, len(peers))
    feats_load.wait()
    sem = take(3)
    near = [send(xg.at[row], xg.at[row], sem + d - 1, dy=d) for d in (1, 2, 3)]
    side_sem = take(4)
    side = [send(xg.at[row], xg.at[row], side_sem, dcore=1)]
    meta_load.wait()
    for copy in tile_loads:
        copy.wait()

    unroll = 16
    quarter = tiles // 4

    def compress(base, acc):
        def some(i, acc):
            for u in range(unroll):
                k = base + i * unroll + u
                c = meta[0, k]
                value = raw[lax.shift_right_logical(c, 1)].astype(f32)
                acc = jnp.where((c & 1) == 1, value, acc + value)
                slots[k] = acc.astype(bf16)
            return acc

        return lax.fori_loop(0, quarter // unroll, some, acc)

    acc = jnp.zeros((BLK, BLK), f32)
    for n in range(4):
        acc = compress(n * quarter, acc)
        if n == 2:
            for d in (1, 2, 3):
                near[d - 1].wait_recv()
                other = lax.rem(y + 4 - d, 4) * 2 + core
                side.append(send(xg.at[other], xg.at[other], side_sem + d, dcore=1))
    for copy in side:
        copy.wait_recv()

    sem_a, sem_b = take(3), take(12)

    def a_copy(q, xq):
        return remote(part.at[xq, 0], recv_a.at[q], sem_a + q, dx=q + 1)

    def b_copy(q, xq, d):
        return remote(
            part.at[xq, 1, lax.rem(z + d, 4)], recv_b.at[d - 1, xq], sem_b + q * 3 + d - 1, dz=d
        )

    def tile(r, c):
        return slots[meta[1, r * 16 + c]]

    def forward(q, carry):
        xq = lax.rem(x + 1 + q, 4)
        lhs = jnp.concatenate(
            [
                jnp.concatenate([tile(2 * (4 * xq + zz) + h, c) for c in range(16)], axis=1)
                for h in range(2)
                for zz in range(4)
            ],
            axis=0,
        )
        source = xg[...].reshape(16 * BLK, BLK)
        product = jnp.dot(lhs, source, preferred_element_type=f32)
        part[xq] = product.astype(bf16).reshape(2, 4, BLK, BLK)

        @pl.when(q < 3)
        def _():
            a_copy(q, xq).start()

        for d in (1, 2, 3):
            b_copy(q, xq, d).start()
        return carry

    lax.fori_loop(0, 4, forward, 0)
    xqs = [lax.rem(x + 1 + q, 4) for q in range(4)]
    for q in range(4):
        if q < 3:
            sent.append(a_copy(q, xqs[q]))
        for d in (1, 2, 3):
            sent.append(b_copy(q, xqs[q], d))

    second_a, second_b = take(3), take(3)
    got_a, got_b = [], []

    def b_sum(q):
        total = part[xqs[q], 1, z].astype(f32)
        for d in (1, 2, 3):
            b_copy(q, xqs[q], d).wait_recv()
            total = total + recv_b[d - 1, xqs[q]].astype(f32)
        return total

    for q in range(3):
        sum_b[q] = b_sum(q).astype(bf16)
        got_b.append(send(sum_b.at[q], recv_b2.at[q], second_b + q, dx=q + 1))
    total = part[x, 0].astype(f32)
    for q in range(3):
        a_copy(q, xqs[q]).wait_recv()
        total = total + recv_a[q].astype(f32)
    sum_a[...] = total.astype(bf16)
    for d in (1, 2, 3):
        got_a.append(send(sum_a.at[lax.rem(z + d, 4)], recv_a2.at[d - 1], second_a + d - 1, dz=d))
    half_b = b_sum(3)
    half_a = sum_a[z].astype(f32)
    for q in range(3):
        got_b[q].wait_recv()
        half_b = half_b + recv_b2[q].astype(f32)
    for q in range(3):
        got_a[q].wait_recv()
        half_a = half_a + recv_a2[q].astype(f32)
    aggregated = jnp.concatenate([half_a, half_b], axis=0)
    agg = aggregated.astype(bf16)

    weight_load.wait()
    cot_load.wait()
    pre = jnp.dot(agg, weight[...], preferred_element_type=f32) + bias_ref[...]
    sigma = jax.nn.sigmoid(pre)
    slope = (cot[...].astype(f32) * sigma * (1.0 + pre * (1.0 - sigma))).astype(bf16)
    vertex = lax.dot_general(
        weight[...], slope, (((1,), (1,)), ((), ())), preferred_element_type=f32
    ).astype(bf16)
    grads[col, 0] = vertex[:, :BLK]
    grads[col, 1] = vertex[:, BLK:]

    sem_ax, sem_bz, sem_az, sem_bx = take(3), take(3), take(3), take(3)
    sem_af, sem_bf = take(9), take(9)
    own_a, own_b = grads.at[col, 0], grads.at[col, 1]
    ax = [send(own_a, own_a, sem_ax + d - 1, dx=d) for d in (1, 2, 3)]
    bz = [send(own_b, own_b, sem_bz + d - 1, dz=d) for d in (1, 2, 3)]
    az = [send(own_a, own_a, sem_az + d - 1, dz=d) for d in (1, 2, 3)]
    bx = [send(own_b, own_b, sem_bx + d - 1, dx=d) for d in (1, 2, 3)]

    out_ref[...] = (pre * sigma).astype(bf16)
    wide = slope.astype(f32)
    bias_part = wide[0:8]
    for n in range(1, wide.shape[0] // 8):
        bias_part = bias_part + wide[n * 8 : n * 8 + 8]
    weight_part = jnp.dot(
        jnp.transpose(agg.astype(f32)).astype(bf16), slope, preferred_element_type=f32
    )

    w_sem1, w_sem2, w_sem3, w_sem4, w_sem5, w_sem6 = (take(n) for n in (3, 3, 1, 3, 3, 3))
    for n in range(4):
        w1[n, 0, 0:32] = weight_part[n * 32 : n * 32 + 32]
        w1[n, 0, 32:40] = bias_part

    def w1_start():
        return [
            send(w1.at[lax.rem(x + d, 4), 0], w1.at[0, d], w_sem1 + d - 1, dx=d)
            for d in (1, 2, 3)
        ]

    def in_order(me, own, received):
        total = None
        for n in range(4):
            term = own
            for d in (1, 2, 3):
                term = jnp.where(lax.rem(me + 4 - d, 4) == n, received[d - 1], term)
            total = term if total is None else total + term
        return total

    w_got1 = w1_start()

    af, bf = {}, {}
    for e in (1, 2, 3):
        ax[e - 1].wait_recv()
        from_x = grads.at[lax.rem(x + 4 - e, 4) * 4 + z, 0]
        for d in (1, 2, 3):
            af[e, d] = send(from_x, from_x, sem_af + (e - 1) * 3 + d - 1, dz=d)
        bz[e - 1].wait_recv()
        from_z = grads.at[x * 4 + lax.rem(z + 4 - e, 4), 1]
        for d in (1, 2, 3):
            bf[e, d] = send(from_z, from_z, sem_bf + (e - 1) * 3 + d - 1, dx=d)

    def group(g):
        zg, xg_ = lax.rem(z + 4 - g, 4), lax.rem(x + 4 - g, 4)
        return [(xx * 4 + zg, 0) for xx in range(4)] + [(xg_ * 4 + zz, 1) for zz in range(4)]

    def backward(g, i):
        members = group(g)
        lhs = jnp.concatenate([grads[j, h] for j, h in members], axis=1)
        rhs = jnp.concatenate(
            [
                jnp.concatenate([tile(2 * j + h, 2 * i + b) for b in range(2)], axis=1)
                for j, h in members
            ],
            axis=0,
        )
        return jnp.dot(lhs, rhs, preferred_element_type=f32)

    def first_group(i, carry):
        back[i] = backward(0, i)
        return carry

    lax.fori_loop(0, 8, first_group, 0)

    for copy in w_got1:
        copy.wait_recv()
    total = in_order(x, w1[x, 0], [w1[0, d] for d in (1, 2, 3)])
    for n in range(4):
        w2[n, 0, 0:8] = total[n * 8 : n * 8 + 8]
        w2[n, 0, 8:16] = total[32:40]
    w_got2 = [
        send(w2.at[lax.rem(z + d, 4), 0], w2.at[0, d], w_sem2 + d - 1, dz=d) for d in (1, 2, 3)
    ]

    def arrive(g):
        az[g - 1].wait_recv()
        bx[g - 1].wait_recv()
        for e in (1, 2, 3):
            af[e, g].wait_recv()
            bf[e, g].wait_recv()

    def add_group(g):
        arrive(g)

        def one(i, carry):
            back[i] += backward(g, i)
            return carry

        lax.fori_loop(0, 8, one, 0)

    add_group(1)

    for copy in w_got2:
        copy.wait_recv()
    w3[0] = in_order(z, w2[z, 0], [w2[0, d] for d in (1, 2, 3)])
    w_got3 = send(w3.at[0], w3.at[1], w_sem3, dcore=1)

    add_group(2)

    w_got3.wait_recv()
    w4[0] = w3[0] + w3[1]
    w_got4 = [send(w4.at[0], w4.at[d], w_sem4 + d - 1, dy=d) for d in (1, 2, 3)]

    arrive(3)
    rs_sem1, rs_sem2 = take(4), take(3)
    order = (1, 2, 3, 0)
    got1 = []
    for n, d in enumerate(order):
        r = lax.rem(y + d, 4) * 2 + (1 - core)
        rs1_out[n] = (back[r] + backward(3, r)).astype(bf16)
        got1.append(send(rs1_out.at[n], rs1_in.at[n], rs_sem1 + n, dcore=1))
    got2 = []
    for n, d in enumerate(order):
        r = lax.rem(y + d, 4) * 2 + core
        total = back[r] + backward(3, r)
        got1[n].wait_recv()
        total = total + rs1_in[n].astype(f32)
        if d:
            rs2_out[n] = total.astype(bf16)
            got2.append(send(rs2_out.at[n], rs2_in.at[n], rs_sem2 + n, dy=d))

    for copy in w_got4:
        copy.wait_recv()
    summed = in_order(y, w4[0], [w4[d] for d in (1, 2, 3)])
    scale = 1.0 / math.sqrt(256 * lax.axis_size("row") * lax.axis_size("col"))
    w5[z] = summed[0:8] * scale
    w_got5 = [send(w5.at[z], w5.at[z], w_sem5 + d - 1, dz=d) for d in (1, 2, 3)]
    bgrad_ref[...] = jnp.sum(summed[8:16], axis=0, keepdims=True) * scale
    for copy in w_got5:
        copy.wait_recv()
    w6[x] = w5[...].reshape(32, 256)
    w_got6 = [send(w6.at[x], w6.at[x], w_sem6 + d - 1, dx=d) for d in (1, 2, 3)]

    for n in range(3):
        got2[n].wait_recv()
        total = total + rs2_in[n].astype(f32)
    fgrad_ref[...] = jnp.transpose(total)
    for copy in w_got6:
        copy.wait_recv()
    wgrad_ref[...] = w6[...].reshape(128, 256)
    for copy in sent:
        copy.wait_send()
    assert counter[0] <= SEMS, counter[0]


SEMS = 96


def local(features, tile_values, tile_coords, tile_count, weight, bias, cotangent):
    tiles = tile_values.shape[2]
    vmem = pl.BlockSpec(memory_space=pltpu.VMEM)
    smem = pl.BlockSpec(memory_space=pltpu.SMEM)
    anywhere = pl.BlockSpec(memory_space=pl.ANY)
    square = (BLK, BLK)
    out, wgrad, bgrad, fgrad = pl.pallas_call(
        kernel,
        name="graph_layer",
        out_shape=(
            jax.ShapeDtypeStruct((256, 256), bf16),
            jax.ShapeDtypeStruct((128, 256), f32),
            jax.ShapeDtypeStruct((1, 256), f32),
            jax.ShapeDtypeStruct((256, 128), f32),
        ),
        in_specs=[anywhere, anywhere, anywhere, smem, anywhere, vmem, anywhere],
        out_specs=(vmem, vmem, vmem, vmem),
        scratch_shapes=[
            pltpu.VMEM((tiles, *square), bf16),
            pltpu.VMEM((tiles + 1, *square), bf16),
            pltpu.VMEM((8, 256, 128), bf16),
            pltpu.VMEM((2, tiles), i32),
            pltpu.VMEM((128, 256), bf16),
            pltpu.VMEM((256, 256), bf16),
            pltpu.VMEM((2, tiles), i32),
            pltpu.SMEM((2, tiles), i32),
            pltpu.VMEM((4, 2, 4, *square), bf16),
            pltpu.VMEM((3, 4, *square), bf16),
            pltpu.VMEM((3, 4, *square), bf16),
            pltpu.VMEM((4, *square), bf16),
            pltpu.VMEM((3, *square), bf16),
            pltpu.VMEM((3, *square), bf16),
            pltpu.VMEM((3, *square), bf16),
            pltpu.VMEM((16, 2, *square), bf16),
            pltpu.VMEM((8, 128, 256), f32),
            pltpu.VMEM((4, 128, 256), bf16),
            pltpu.VMEM((4, 128, 256), bf16),
            pltpu.VMEM((3, 128, 256), bf16),
            pltpu.VMEM((3, 128, 256), bf16),
            pltpu.VMEM((4, 4, 40, 256), f32),
            pltpu.VMEM((4, 4, 16, 256), f32),
            pltpu.VMEM((2, 16, 256), f32),
            pltpu.VMEM((4, 16, 256), f32),
            pltpu.VMEM((4, 8, 256), f32),
            pltpu.VMEM((4, 32, 256), f32),
            pltpu.SemaphoreType.DMA((4 + LOADS,)),
            pltpu.SemaphoreType.DMA((SEMS,)),
            pltpu.SemaphoreType.DMA((SEMS,)),
        ],
        compiler_params=pltpu.CompilerParams(
            collective_id=0, has_side_effects=True, vmem_limit_bytes=56 * 2**20
        ),
    )(features, tile_values, tile_coords, tile_count, weight, bias.reshape(1, 256), cotangent)
    return out, wgrad, bgrad.reshape(256), fgrad


def solution(mesh):
    placed = (
        P(("row", "col"), None),
        P("row", "col", None, None, None),
        P("row", "col", None, None),
        P("row", "col"),
        P(),
        P(),
        P(("row", "col"), None),
    )
    return jax.shard_map(
        local,
        mesh=mesh,
        in_specs=placed,
        out_specs=(P(("row", "col"), None), P(), P(), P(("row", "col"), None)),
        check_vma=False,
    )
```

time: 425 us -> 65.8 us (0.15)
  the two profiles are of different devices: /device:TPU:1 before, /device:TPU:0 now
where the time goes in v1:
time: 65.8 us; the launch traced here: 65.6 us
  Pallas kernels  58.4 us (89%)
  local copies, waits for them, and re-layouts  5.89 us (9%)
  between operations  1.29 us (2%)
    pallas_call x1, Pallas kernels, local(): pl.pallas_call(kernel, name='graph_layer', out_shape=(jax.ShapeDtypeStruc...  58.4 us
    unnamed x4, local copies, waits for them, and re-layouts  5.89 us

profile of v1, /device:TPU:0, one launch (start us, length us, event | category | flops | bytes accessed | tf_op | source)
XLA Modules:
  0.0 65.6 jit_solution(6949435811627636629)
XLA Ops:
  1.3 58.4 %graph_layer.1 = (bf16[256,256]{1,0:T(8,128)(2,1)}, f32[128,256]{1,0:T(8,128)}, f32[1,256]{1,0:T(1,128)}, f32[256,128]{1,0:T(8,128)}) custom-call(bf16[256,128]{1,0:T(8,128)(2,1)} %feats_hbm.1, bf16[1,1,512,128,128]{4,3,2,1,0:T(8,128)(2,1)} %tiles_hbm.1, s32[1,1,2,512]{3,2,1,0:T(2,128)} %coords_hbm.1, s32[1,1]{1,0:T(1,128)S(6)} %copy.15.count_ref, ...), custom_call_target="tpu_custom_call" | custom-call | tf_op jit(solution)/shard_map/graph_layer/pallas_call | solution.py:403
  59.7 1.6 %copy.16 = bf16[256,256]{1,0:T(8,128)(2,1)} copy(bf16[256,256]{1,0:T(8,128)(2,1)} %get-tuple-element.16) | data formatting | bytes 262144
  61.3 1.6 %copy.17 = f32[128,256]{1,0:T(8,128)} copy(f32[128,256]{1,0:T(8,128)} %get-tuple-element.17) | data formatting | bytes 262144
  62.9 1.2 %copy.18 = f32[256]{0:T(256)} copy(f32[256]{0:T(256)} %bitcast.3) | data formatting | bytes 2048
  64.1 1.6 %copy.19 = f32[256,128]{1,0:T(8,128)} copy(f32[256,128]{1,0:T(8,128)} %get-tuple-element.19) | data formatting | bytes 262144

commit v2 on v1

v2 whole, which is shorter than its diff:
```python
import functools
import math

import jax
import jax.numpy as jnp
from jax import lax
from jax.experimental import pallas as pl
from jax.experimental.pallas import tpu as pltpu
from jax.sharding import PartitionSpec as P

f32, bf16, i32 = jnp.float32, jnp.bfloat16, jnp.int32
MESH = pl.DeviceIdType.MESH
BLK = 128


def kernel(
    feats_hbm, tiles_hbm, coords_hbm, count_hbm, weight_hbm, bias_hbm, cot_hbm,
    out_ref, wgrad_ref, bgrad_ref, fgrad_ref,
    raw0, raw1, slots, seeds, xg, coords, alive, weight, bias, cot, meta_v, meta,
    part, recv_a, recv_b, sum_a, sum_b, recv_a2, recv_b2,
    grads, back, rs1_out, rs1_in, rs2_out, rs2_in,
    w1, w2, w3, w4, w5,
    load_sem, send_sem, recv_sem,
):
    raws = (raw0, raw1)
    tiles = 2 * raw0.shape[0]
    row, col = lax.axis_index("row"), lax.axis_index("col")
    y, core = lax.div(row, 2), lax.rem(row, 2)
    x, z = lax.div(col, 4), lax.rem(col, 4)

    def device(dy=0, dcore=0, dx=0, dz=0):
        return (
            lax.rem(y + dy, 4) * 2 + lax.rem(core + dcore, 2),
            lax.rem(x + dx, 4) * 4 + lax.rem(z + dz, 4),
        )

    counter = [0]

    def remote(src, dst, sem, **where):
        return pltpu.make_async_remote_copy(
            src_ref=src,
            dst_ref=dst,
            send_sem=send_sem.at[sem],
            recv_sem=recv_sem.at[sem],
            device_id=device(**where),
            device_id_type=MESH,
        )

    def take(count):
        first = counter[0]
        counter[0] += count
        return first

    sent = []

    def send(*args, **where):
        copy = remote(*args, **where)
        copy.start()
        sent.append(copy)
        return copy

    def load(src, dst, sem):
        copy = pltpu.make_async_copy(src, dst, load_sem.at[sem])
        copy.start()
        return copy

    half = tiles // 2
    coords_load = load(coords_hbm.at[0, 0], coords, 0)
    count_load = load(count_hbm, alive, 1)
    feats_load = load(feats_hbm, xg.at[row], 2)
    tile_loads = [
        load(tiles_hbm.at[0, 0, pl.ds(n * half, half)], raws[n], 3 + n)
        for n in range(2)
    ]
    weight_load = load(weight_hbm, weight, 5)
    bias_load = load(bias_hbm, bias, 6)
    cot_load = load(cot_hbm, cot, 7)

    barrier = pltpu.get_barrier_semaphore()
    peers = [device(dcore=1)]
    for d in (1, 2, 3):
        peers += [device(dy=d), device(dx=d), device(dz=d)]
    for peer in peers:
        pl.semaphore_signal(barrier, inc=1, device_id=peer, device_id_type=MESH)

    slots[tiles] = jnp.zeros((BLK, BLK), bf16)
    seeds[half] = jnp.zeros((BLK, BLK), bf16)
    coords_load.wait()
    count_load.wait()
    lanes = lax.broadcasted_iota(i32, (1, tiles), 1)
    pos = jnp.where(lanes < alive[...], coords[0:1, :] * 16 + coords[1:2, :], tiles)

    def down(v):
        return jnp.transpose(jnp.broadcast_to(v, (BLK, v.shape[1])))

    def count(mask):
        return jnp.sum(jnp.where(mask, 1, 0), axis=0, keepdims=True)

    key = pos * tiles + lanes
    ranks, firsts = [], []
    pos_down, key_down = down(pos), down(key)
    for n in range(tiles // BLK):
        cut = slice(n * BLK, (n + 1) * BLK)
        same = slice(0, half) if n < tiles // BLK // 2 else slice(half, tiles)
        before = key_down[same] < key[:, cut]
        ranks.append(count(before))
        firsts.append(count(before & (pos_down[same] == pos[:, cut])))

    pl.semaphore_wait(barrier, len(peers))
    feats_load.wait()
    sem = take(3)
    near = [send(xg.at[row], xg.at[row], sem + d - 1, dy=d) for d in (1, 2, 3)]
    side_sem = take(4)
    side = [send(xg.at[row], xg.at[row], side_sem, dcore=1)]

    rank = jnp.concatenate(ranks, axis=1)
    first = jnp.where(jnp.concatenate(firsts, axis=1) == 0, 1, 0)
    seed = []
    for n in range(tiles // BLK):
        cut = slice(n * BLK, (n + 1) * BLK)
        if n < tiles // BLK // 2:
            seed.append(jnp.full((1, BLK), half, i32))
        else:
            upto, here = count(pos_down[:half] <= pos[:, cut]), count(pos_down[:half] == pos[:, cut])
            seed.append(jnp.where(here == 0, half, upto - 1))
    code = (jnp.concatenate(seed, axis=1) * tiles + lanes) * 2 + first
    rank_down, code_down = down(rank), down(code)
    for n in range(tiles // BLK):
        cut = slice(n * BLK, (n + 1) * BLK)
        at = lanes[:, cut]
        same = slice(0, half) if n < tiles // BLK // 2 else slice(half, tiles)
        slot = at if n < tiles // BLK // 2 else at - half
        meta_v[0:1, cut] = jnp.sum(
            jnp.where(rank_down[same] == slot, code_down[same], 0), axis=0, keepdims=True
        )
        upto0, here0 = count(pos_down[:half] <= at), count(pos_down[:half] == at)
        upto1, here1 = count(pos_down[half:] <= at), count(pos_down[half:] == at)
        early = jnp.where(here0 == 0, tiles, upto0 - 1)
        meta_v[1:2, cut] = jnp.where(here1 == 0, early, half + upto1 - 1)
    meta_load = load(meta_v, meta, 0)
    meta_load.wait()

    unroll = 16

    def compress(base, size, seeded, acc):
        def some(i, acc):
            for u in range(unroll):
                k = base + i * unroll + u
                c = meta[0, k]
                value = raws[seeded][lax.shift_right_logical(c, 1) & (half - 1)].astype(f32)
                begins = (c & 1) == 1
                if seeded:
                    begin = seeds[lax.shift_right_logical(c, 10)].astype(f32)
                    acc = jnp.where(begins, begin, acc) + value
                    slots[k] = acc.astype(bf16)
                else:
                    acc = jnp.where(begins, value, acc + value)
                    slots[k] = acc.astype(bf16)
                    seeds[k] = acc.astype(bf16)
            return acc

        return lax.fori_loop(0, size // unroll, some, acc)

    tile_loads[0].wait()
    acc = compress(0, half, False, jnp.zeros((BLK, BLK), f32))
    tile_loads[1].wait()
    quarter = half // 4
    for n in range(4):
        acc = compress(half + n * quarter, quarter, True, acc)
        for d in ((), (), (1, 3), (2,))[n]:
            near[d - 1].wait_recv()
            other = lax.rem(y + 4 - d, 4) * 2 + core
            side.append(send(xg.at[other], xg.at[other], side_sem + d, dcore=1))
    for copy in side:
        copy.wait_recv()

    sem_a, sem_b = take(12), take(12)

    def a_copy(q, xq, d):
        zt = lax.rem(z + d, 4)
        return remote(part.at[xq, 0, zt], recv_a.at[q, zt], sem_a + q * 4 + d, dx=q + 1)

    def b_copy(q, xq, d):
        return remote(
            part.at[xq, 1, lax.rem(z + d, 4)], recv_b.at[d - 1, xq], sem_b + q * 3 + d - 1, dz=d
        )

    def tile(r, c):
        return slots[meta[1, r * 16 + c]]

    def forward(q, carry):
        xq = lax.rem(x + 1 + q, 4)
        lhs = jnp.concatenate(
            [
                jnp.concatenate([tile(2 * (4 * xq + zz) + h, c) for c in range(16)], axis=1)
                for h in range(2)
                for zz in range(4)
            ],
            axis=0,
        )
        source = xg[...].reshape(16 * BLK, BLK)
        product = jnp.dot(lhs, source, preferred_element_type=f32)
        part[xq] = product.astype(bf16).reshape(2, 4, BLK, BLK)

        @pl.when(q < 3)
        def _():
            for d in (1, 2, 3, 0):
                a_copy(q, xq, d).start()

        for d in (1, 2, 3):
            b_copy(q, xq, d).start()
        return carry

    lax.fori_loop(0, 4, forward, 0)
    xqs = [lax.rem(x + 1 + q, 4) for q in range(4)]
    for q in range(4):
        if q < 3:
            for d in range(4):
                sent.append(a_copy(q, xqs[q], d))
        for d in (1, 2, 3):
            sent.append(b_copy(q, xqs[q], d))

    second_a, second_b = take(3), take(3)
    got_a, got_b = [], []

    def b_sum(q):
        total = part[xqs[q], 1, z].astype(f32)
        for d in (1, 2, 3):
            b_copy(q, xqs[q], d).wait_recv()
            total = total + recv_b[d - 1, xqs[q]].astype(f32)
        return total

    for q in range(3):
        sum_b[q] = b_sum(q).astype(bf16)
        got_b.append(send(sum_b.at[q], recv_b2.at[q], second_b + q, dx=q + 1))

    def a_sum(d):
        zt = lax.rem(z + d, 4)
        total = part[x, 0, zt].astype(f32)
        for q in range(3):
            a_copy(q, xqs[q], d).wait_recv()
            total = total + recv_a[q, zt].astype(f32)
        return total

    for d in (1, 2, 3):
        sum_a[d - 1] = a_sum(d).astype(bf16)
        got_a.append(send(sum_a.at[d - 1], recv_a2.at[d - 1], second_a + d - 1, dz=d))
    half_b = b_sum(3)
    half_a = a_sum(0)
    for q in range(3):
        got_b[q].wait_recv()
        half_b = half_b + recv_b2[q].astype(f32)
    for q in range(3):
        got_a[q].wait_recv()
        half_a = half_a + recv_a2[q].astype(f32)
    aggregated = jnp.concatenate([half_a, half_b], axis=0)
    agg = aggregated.astype(bf16)

    weight_load.wait()
    bias_load.wait()
    cot_load.wait()
    pre = jnp.dot(agg, weight[...], preferred_element_type=f32) + bias[...]
    sigma = jax.nn.sigmoid(pre)
    slope = (cot[...].astype(f32) * sigma * (1.0 + pre * (1.0 - sigma))).astype(bf16)
    vertex = lax.dot_general(
        weight[...], slope, (((1,), (1,)), ((), ())), preferred_element_type=f32
    ).astype(bf16)
    grads[col, 0] = vertex[:, :BLK]
    grads[col, 1] = vertex[:, BLK:]

    sem_ax, sem_bz, sem_az, sem_bx = take(3), take(3), take(3), take(3)
    sem_af, sem_bf = take(9), take(9)
    own_a, own_b = grads.at[col, 0], grads.at[col, 1]
    ax, bz, az, bx = {}, {}, {}, {}
    near_first = (1, 3, 2)
    for d in near_first:
        ax[d] = send(own_a, own_a, sem_ax + d - 1, dx=d)
        bz[d] = send(own_b, own_b, sem_bz + d - 1, dz=d)
    for d in near_first:
        az[d] = send(own_a, own_a, sem_az + d - 1, dz=d)
        bx[d] = send(own_b, own_b, sem_bx + d - 1, dx=d)

    wide = slope.astype(f32)
    bias_part = wide[0:8]
    for n in range(1, wide.shape[0] // 8):
        bias_part = bias_part + wide[n * 8 : n * 8 + 8]
    weight_part = jnp.dot(
        jnp.transpose(agg.astype(f32)).astype(bf16), slope, preferred_element_type=f32
    )
    w_sem1, w_sem2, w_sem3, w_sem4, w_sem5, w_sem6 = (take(n) for n in (1, 3, 3, 3, 3, 1))
    for n in range(2):
        w1[n, 0:64] = weight_part[n * 64 : n * 64 + 64]
        w1[n, 64:72] = bias_part
    w_got1 = send(w1.at[1 - core], w1.at[2], w_sem1, dcore=1)
    out_ref[...] = (pre * sigma).astype(bf16)

    def in_order(me, own, received):
        total = None
        for n in range(4):
            term = own
            for d in (1, 2, 3):
                term = jnp.where(lax.rem(me + 4 - d, 4) == n, received[d - 1], term)
            total = term if total is None else total + term
        return total

    w_got1.wait_recv()
    pair = w1[core] + w1[2]
    for n in range(4):
        w2[n, 0:16] = pair[n * 16 : n * 16 + 16]
        w2[n, 16:24] = pair[64:72]
    w_got2 = [
        send(w2.at[lax.rem(y + d, 4)], w2.at[3 + d], w_sem2 + d - 1, dy=d) for d in (1, 2, 3)
    ]

    af, bf = {}, {}
    for e in near_first:
        ax[e].wait_recv()
        bz[e].wait_recv()
    for d in near_first:
        for e in near_first:
            from_x = grads.at[lax.rem(x + 4 - e, 4) * 4 + z, 0]
            from_z = grads.at[x * 4 + lax.rem(z + 4 - e, 4), 1]
            af[e, d] = send(from_x, from_x, sem_af + (e - 1) * 3 + d - 1, dz=d)
            bf[e, d] = send(from_z, from_z, sem_bf + (e - 1) * 3 + d - 1, dx=d)

    for copy in w_got2:
        copy.wait_recv()
    w3[0] = in_order(y, w2[y], [w2[3 + d] for d in (1, 2, 3)])
    w_got3 = [send(w3.at[0], w3.at[d], w_sem3 + d - 1, dx=d) for d in (1, 2, 3)]

    def group(g):
        zg, xg_ = lax.rem(z + 4 - g, 4), lax.rem(x + 4 - g, 4)
        return [(xx * 4 + zg, 0) for xx in range(4)] + [(xg_ * 4 + zz, 1) for zz in range(4)]

    def backward(g, i):
        members = group(g)
        lhs = jnp.concatenate([grads[j, h] for j, h in members], axis=1)
        rhs = jnp.concatenate(
            [
                jnp.concatenate([tile(2 * j + h, 2 * i + b) for b in range(2)], axis=1)
                for j, h in members
            ],
            axis=0,
        )
        return jnp.dot(lhs, rhs, preferred_element_type=f32)

    WIDE = 4

    def run_group(g, fresh):
        def some(m, carry):
            for u in range(WIDE):
                i = m * WIDE + u
                back[i] = backward(g, i) if fresh else back[i] + backward(g, i)
            return carry

        lax.fori_loop(0, 8 // WIDE, some, 0)

    def arrive(g):
        az[g].wait_recv()
        bx[g].wait_recv()
        for e in (1, 2, 3):
            af[e, g].wait_recv()
            bf[e, g].wait_recv()

    run_group(0, True)
    arrive(1)
    run_group(1, False)
    arrive(3)

    for copy in w_got3:
        copy.wait_recv()
    w4[0] = in_order(x, w3[0], [w3[d] for d in (1, 2, 3)])
    w_got4 = [send(w4.at[0], w4.at[d], w_sem4 + d - 1, dz=d) for d in (1, 2, 3)]
    run_group(3, False)

    arrive(2)
    rs_sem1, rs_sem2 = take(4), take(3)
    order = (2, 1, 3, 0)
    got1 = []
    for n, d in enumerate(order):
        r = lax.rem(y + d, 4) * 2 + (1 - core)
        rs1_out[n] = (back[r] + backward(2, r)).astype(bf16)
        got1.append(send(rs1_out.at[n], rs1_in.at[n], rs_sem1 + n, dcore=1))
    got2 = []
    own = []
    for d in order:
        r = lax.rem(y + d, 4) * 2 + core
        own.append(back[r] + backward(2, r))
    for n, d in enumerate(order):
        got1[n].wait_recv()
        total = own[n] + rs1_in[n].astype(f32)
        if d:
            rs2_out[n] = total.astype(bf16)
            got2.append(send(rs2_out.at[n], rs2_in.at[n], rs_sem2 + n, dy=d))

    for copy in w_got4:
        copy.wait_recv()
    summed = in_order(z, w4[0], [w4[d] for d in (1, 2, 3)])
    scale = 1.0 / math.sqrt(256 * lax.axis_size("row") * lax.axis_size("col"))
    w5[core, y] = summed[0:16] * scale
    w_got5 = [send(w5.at[core, y], w5.at[core, y], w_sem5 + d - 1, dy=d) for d in (1, 2, 3)]
    bgrad_ref[...] = jnp.sum(summed[16:24], axis=0, keepdims=True) * scale
    for copy in w_got5:
        copy.wait_recv()
    w_got6 = send(w5.at[core], w5.at[core], w_sem6, dcore=1)

    for n in range(3):
        got2[n].wait_recv()
        total = total + rs2_in[n].astype(f32)
    fgrad_ref[...] = jnp.transpose(total)
    w_got6.wait_recv()
    wgrad_ref[...] = w5[...].reshape(128, 256)
    for copy in sent:
        copy.wait_send()
    assert counter[0] <= SEMS, counter[0]


SEMS = 112


def local(features, tile_values, tile_coords, tile_count, weight, bias, cotangent):
    tiles = tile_values.shape[2]
    vmem = pl.BlockSpec(memory_space=pltpu.VMEM)
    anywhere = pl.BlockSpec(memory_space=pl.ANY)
    square = (BLK, BLK)
    out, wgrad, bgrad, fgrad = pl.pallas_call(
        kernel,
        name="graph_layer",
        out_shape=(
            pltpu.VMEM((256, 256), bf16),
            pltpu.VMEM((128, 256), f32),
            pltpu.VMEM((1, 256), f32),
            pltpu.VMEM((256, 128), f32),
        ),
        in_specs=[pl.BlockSpec(memory_space=pltpu.HBM)] * 7,
        out_specs=(vmem, vmem, vmem, vmem),
        scratch_shapes=[
            pltpu.VMEM((tiles // 2, *square), bf16),
            pltpu.VMEM((tiles // 2, *square), bf16),
            pltpu.VMEM((tiles + 1, *square), bf16),
            pltpu.VMEM((tiles // 2 + 1, *square), bf16),
            pltpu.VMEM((8, 256, 128), bf16),
            pltpu.VMEM((2, tiles), i32),
            pltpu.VMEM((1, 1), i32),
            pltpu.VMEM((128, 256), bf16),
            pltpu.VMEM((1, 256), f32),
            pltpu.VMEM((256, 256), bf16),
            pltpu.VMEM((2, tiles), i32),
            pltpu.SMEM((2, tiles), i32),
            pltpu.VMEM((4, 2, 4, *square), bf16),
            pltpu.VMEM((3, 4, *square), bf16),
            pltpu.VMEM((3, 4, *square), bf16),
            pltpu.VMEM((3, *square), bf16),
            pltpu.VMEM((3, *square), bf16),
            pltpu.VMEM((3, *square), bf16),
            pltpu.VMEM((3, *square), bf16),
            pltpu.VMEM((16, 2, *square), bf16),
            pltpu.VMEM((8, 128, 256), f32),
            pltpu.VMEM((4, 128, 256), bf16),
            pltpu.VMEM((4, 128, 256), bf16),
            pltpu.VMEM((3, 128, 256), bf16),
            pltpu.VMEM((3, 128, 256), bf16),
            pltpu.VMEM((3, 72, 256), f32),
            pltpu.VMEM((7, 24, 256), f32),
            pltpu.VMEM((4, 24, 256), f32),
            pltpu.VMEM((4, 24, 256), f32),
            pltpu.VMEM((2, 4, 16, 256), f32),
            pltpu.SemaphoreType.DMA((8,)),
            pltpu.SemaphoreType.DMA((SEMS,)),
            pltpu.SemaphoreType.DMA((SEMS,)),
        ],
        compiler_params=pltpu.CompilerParams(
            collective_id=0, has_side_effects=True, vmem_limit_bytes=56 * 2**20
        ),
    )(features, tile_values, tile_coords, tile_count, weight, bias.reshape(1, 256), cotangent)
    kinds = (((256, 256), bf16), ((128, 256), f32), ((1, 256), f32), ((256, 128), f32))
    out, wgrad, bgrad, fgrad = pl.pallas_call(
        finish,
        name="finish",
        out_shape=[jax.ShapeDtypeStruct(*kind) for kind in kinds],
        in_specs=[anywhere] * 4,
        out_specs=[anywhere] * 4,
        scratch_shapes=[pltpu.SemaphoreType.DMA((4,))],
    )(*(pltpu.with_memory_space_constraint(v, pltpu.VMEM) for v in (out, wgrad, bgrad, fgrad)))
    return out, wgrad, bgrad.reshape(256), fgrad


def finish(*refs):
    sems = refs[-1]
    copies = [pltpu.make_async_copy(refs[n], refs[4 + n], sems.at[n]) for n in range(4)]
    for copy in copies:
        copy.start()
    for copy in copies:
        copy.wait()


def solution(mesh):
    placed = (
        P(("row", "col"), None),
        P("row", "col", None, None, None),
        P("row", "col", None, None),
        P("row", "col"),
        P(),
        P(),
        P(("row", "col"), None),
    )
    return jax.shard_map(
        local,
        mesh=mesh,
        in_specs=placed,
        out_specs=(P(("row", "col"), None), P(), P(), P(("row", "col"), None)),
        check_vma=False,
    )
```

time: 65.8 us -> 54.4 us (0.83)
  the two profiles are of different devices: /device:TPU:0 before, /device:TPU:1 now
where the time goes in v2:
time: 54.4 us; the launch traced here: 54.3 us
  Pallas kernels  53 us (97%)
  between operations  1.29 us (2%)
    pallas_call x1, Pallas kernels, local(): pl.pallas_call(kernel, name='graph_layer', out_shape=(pltpu.VMEM((256, 25...  52.2 us

profile of v2, /device:TPU:1, one launch (start us, length us, event | category | flops | bytes accessed | tf_op | source)
XLA Modules:
  0.0 54.3 jit_solution(5221658205042270702)
XLA Ops:
  1.3 52.2 %graph_layer.1 = (bf16[256,256]{1,0:T(8,128)(2,1)S(1)}, f32[128,256]{1,0:T(8,128)S(1)}, f32[1,256]{1,0:T(1,128)S(1)}, f32[256,128]{1,0:T(8,128)S(1)}) custom-call(bf16[256,128]{1,0:T(8,128)(2,1)} %feats_hbm.1, bf16[1,1,512,128,128]{4,3,2,1,0:T(8,128)(2,1)} %tiles_hbm.1, s32[1,1,2,512]{3,2,1,0:T(2,128)} %coords_hbm.1, s32[1,1]{1,0:T(1,128)S(6)} %copy.11.count_hbm, ...), custom_call_target="tpu_custom_call" | custom-call | tf_op jit(solution)/shard_map/graph_layer/pallas_call | solution.py:426
  53.5 0.8 %finish.1 = (bf16[256,256]{1,0:T(8,128)(2,1)}, f32[128,256]{1,0:T(8,128)}, f32[1,256]{1,0:T(1,128)}, f32[256,128]{1,0:T(8,128)}) custom-call(bf16[256,256]{1,0:T(8,128)(2,1)S(1)} %get-tuple-element.12.refs_0_, f32[128,256]{1,0:T(8,128)S(1)} %get-tuple-element.13.refs_1_, f32[1,256]{1,0:T(1,128)S(1)} %get-tuple-element.14.refs_2_, ...), custom_call_target="tpu_custom_call" | custom-call | tf_op jit(solution)/shard_map/finish/pallas_call | solution.py:477

commit v3 on v2

--- a/solution.py
+++ b/solution.py
@@ -105,13 +105,6 @@
         before = key_down[same] < key[:, cut]
         ranks.append(count(before))
         firsts.append(count(before & (pos_down[same] == pos[:, cut])))
-
-    pl.semaphore_wait(barrier, len(peers))
-    feats_load.wait()
-    sem = take(3)
-    near = [send(xg.at[row], xg.at[row], sem + d - 1, dy=d) for d in (1, 2, 3)]
-    side_sem = take(4)
-    side = [send(xg.at[row], xg.at[row], side_sem, dcore=1)]
 
     rank = jnp.concatenate(ranks, axis=1)
     first = jnp.where(jnp.concatenate(firsts, axis=1) == 0, 1, 0)
@@ -162,23 +155,36 @@
         return lax.fori_loop(0, size // unroll, some, acc)
 
     tile_loads[0].wait()
-    acc = compress(0, half, False, jnp.zeros((BLK, BLK), f32))
+    early = half // 2
+    acc = compress(0, early, False, jnp.zeros((BLK, BLK), f32))
+
+    pl.semaphore_wait(barrier, len(peers))
+    feats_load.wait()
+    sem = take(3)
+    near = [send(xg.at[row], xg.at[row], sem + d - 1, dy=d) for d in (1, 2, 3)]
+    side_sem = take(4)
+    side = [send(xg.at[row], xg.at[row], side_sem, dcore=1)]
+
+    acc = compress(early, half - early, False, acc)
     tile_loads[1].wait()
-    quarter = half // 4
-    for n in range(4):
-        acc = compress(half + n * quarter, quarter, True, acc)
-        for d in ((), (), (1, 3), (2,))[n]:
-            near[d - 1].wait_recv()
-            other = lax.rem(y + 4 - d, 4) * 2 + core
-            side.append(send(xg.at[other], xg.at[other], side_sem + d, dcore=1))
+    compress(half, half, True, acc)
+    for d in (1, 3, 2):
+        near[d - 1].wait_recv()
+        other = lax.rem(y + 4 - d, 4) * 2 + core
+        side.append(send(xg.at[other], xg.at[other], side_sem + d, dcore=1))
     for copy in side:
         copy.wait_recv()
 
     sem_a, sem_b = take(12), take(12)
 
+    def turn(q):
+        if isinstance(q, int):
+            return (2, 1, 3, 0)[q]
+        return 2 - q + 3 * lax.div(q, 2) - 2 * lax.div(q, 3)
+
     def a_copy(q, xq, d):
         zt = lax.rem(z + d, 4)
-        return remote(part.at[xq, 0, zt], recv_a.at[q, zt], sem_a + q * 4 + d, dx=q + 1)
+        return remote(part.at[xq, 0, zt], recv_a.at[q, zt], sem_a + q * 4 + d, dx=turn(q))
 
     def b_copy(q, xq, d):
         return remote(
@@ -189,7 +195,7 @@
         return slots[meta[1, r * 16 + c]]
 
     def forward(q, carry):
-        xq = lax.rem(x + 1 + q, 4)
+        xq = lax.rem(x + turn(q), 4)
         lhs = jnp.concatenate(
             [
                 jnp.concatenate([tile(2 * (4 * xq + zz) + h, c) for c in range(16)], axis=1)
@@ -212,7 +218,7 @@
         return carry
 
     lax.fori_loop(0, 4, forward, 0)
-    xqs = [lax.rem(x + 1 + q, 4) for q in range(4)]
+    xqs = [lax.rem(x + turn(q), 4) for q in range(4)]
     for q in range(4):
         if q < 3:
             for d in range(4):
@@ -232,7 +238,7 @@
 
     for q in range(3):
         sum_b[q] = b_sum(q).astype(bf16)
-        got_b.append(send(sum_b.at[q], recv_b2.at[q], second_b + q, dx=q + 1))
+        got_b.append(send(sum_b.at[q], recv_b2.at[q], second_b + q, dx=turn(q)))
 
     def a_sum(d):
         zt = lax.rem(z + d, 4)
@@ -316,17 +322,22 @@
     for e in near_first:
         ax[e].wait_recv()
         bz[e].wait_recv()
-    for d in near_first:
+
+    def forward_to(d):
         for e in near_first:
             from_x = grads.at[lax.rem(x + 4 - e, 4) * 4 + z, 0]
             from_z = grads.at[x * 4 + lax.rem(z + 4 - e, 4), 1]
             af[e, d] = send(from_x, from_x, sem_af + (e - 1) * 3 + d - 1, dz=d)
             bf[e, d] = send(from_z, from_z, sem_bf + (e - 1) * 3 + d - 1, dx=d)
 
+    forward_to(1)
+    forward_to(3)
+
     for copy in w_got2:
         copy.wait_recv()
     w3[0] = in_order(y, w2[y], [w2[3 + d] for d in (1, 2, 3)])
     w_got3 = [send(w3.at[0], w3.at[d], w_sem3 + d - 1, dx=d) for d in (1, 2, 3)]
+    forward_to(2)
 
     def group(g):
         zg, xg_ = lax.rem(z + 4 - g, 4), lax.rem(x + 4 - g, 4)
@@ -364,13 +375,15 @@
 
     run_group(0, True)
     arrive(1)
+
     run_group(1, False)
-    arrive(3)
 
     for copy in w_got3:
         copy.wait_recv()
     w4[0] = in_order(x, w3[0], [w3[d] for d in (1, 2, 3)])
     w_got4 = [send(w4.at[0], w4.at[d], w_sem4 + d - 1, dz=d) for d in (1, 2, 3)]
+
+    arrive(3)
     run_group(3, False)
 
     arrive(2)
@@ -381,6 +394,14 @@
         r = lax.rem(y + d, 4) * 2 + (1 - core)
         rs1_out[n] = (back[r] + backward(2, r)).astype(bf16)
         got1.append(send(rs1_out.at[n], rs1_in.at[n], rs_sem1 + n, dcore=1))
+    for copy in w_got4:
+        copy.wait_recv()
+    summed = in_order(z, w4[0], [w4[d] for d in (1, 2, 3)])
+    scale = 1.0 / math.sqrt(256 * lax.axis_size("row") * lax.axis_size("col"))
+    w5[core, y] = summed[0:16] * scale
+    w_got5 = [send(w5.at[core, y], w5.at[core, y], w_sem5 + d - 1, dy=d) for d in (1, 2, 3)]
+    bgrad_ref[...] = jnp.sum(summed[16:24], axis=0, keepdims=True) * scale
+
     got2 = []
     own = []
     for d in order:
@@ -393,13 +414,6 @@
             rs2_out[n] = total.astype(bf16)
             got2.append(send(rs2_out.at[n], rs2_in.at[n], rs_sem2 + n, dy=d))
 
-    for copy in w_got4:
-        copy.wait_recv()
-    summed = in_order(z, w4[0], [w4[d] for d in (1, 2, 3)])
-    scale = 1.0 / math.sqrt(256 * lax.axis_size("row") * lax.axis_size("col"))
-    w5[core, y] = summed[0:16] * scale
-    w_got5 = [send(w5.at[core, y], w5.at[core, y], w_sem5 + d - 1, dy=d) for d in (1, 2, 3)]
-    bgrad_ref[...] = jnp.sum(summed[16:24], axis=0, keepdims=True) * scale
     for copy in w_got5:
         copy.wait_recv()
     w_got6 = send(w5.at[core], w5.at[core], w_sem6, dcore=1)

time: 54.4 us -> 53 us (0.974)
  Pallas kernels: 53 us -> 51.6 us
    pallas_call x1, Pallas kernels: 52.2 us -> 50.8 us  [local(): pl.pallas_call(kernel, name='graph_layer', out_shape=(pltpu.VMEM((256, 25...]
where the time goes in v3:
time: 53 us; the launch traced here: 52.9 us
  Pallas kernels  51.6 us (97%)
  between operations  1.29 us (2%)
    pallas_call x1, Pallas kernels, local(): pl.pallas_call(kernel, name='graph_layer', out_shape=(pltpu.VMEM((256, 25...  50.8 us

profile of v3, /device:TPU:1, one launch (start us, length us, event | category | flops | bytes accessed | tf_op | source)
XLA Modules:
  0.0 52.9 jit_solution(15115704481800022861)
XLA Ops:
  1.3 50.8 %graph_layer.1 = (bf16[256,256]{1,0:T(8,128)(2,1)S(1)}, f32[128,256]{1,0:T(8,128)S(1)}, f32[1,256]{1,0:T(1,128)S(1)}, f32[256,128]{1,0:T(8,128)S(1)}) custom-call(bf16[256,128]{1,0:T(8,128)(2,1)} %feats_hbm.1, bf16[1,1,512,128,128]{4,3,2,1,0:T(8,128)(2,1)} %tiles_hbm.1, s32[1,1,2,512]{3,2,1,0:T(2,128)} %coords_hbm.1, s32[1,1]{1,0:T(1,128)S(6)} %copy.11.count_hbm, ...), custom_call_target="tpu_custom_call" | custom-call | tf_op jit(solution)/shard_map/graph_layer/pallas_call | solution.py:440
  52.1 0.8 %finish.1 = (bf16[256,256]{1,0:T(8,128)(2,1)}, f32[128,256]{1,0:T(8,128)}, f32[1,256]{1,0:T(1,128)}, f32[256,128]{1,0:T(8,128)}) custom-call(bf16[256,256]{1,0:T(8,128)(2,1)S(1)} %get-tuple-element.12.refs_0_, f32[128,256]{1,0:T(8,128)S(1)} %get-tuple-element.13.refs_1_, f32[1,256]{1,0:T(1,128)S(1)} %get-tuple-element.14.refs_2_, ...), custom_call_target="tpu_custom_call" | custom-call | tf_op jit(solution)/shard_map/finish/pallas_call | solution.py:491

commit v4 on v3

--- a/solution.py
+++ b/solution.py
@@ -79,7 +79,7 @@
     barrier = pltpu.get_barrier_semaphore()
     peers = [device(dcore=1)]
     for d in (1, 2, 3):
-        peers += [device(dy=d), device(dx=d), device(dz=d)]
+        peers += [device(dy=d), device(dy=d, dcore=1), device(dx=d), device(dz=d)]
     for peer in peers:
         pl.semaphore_signal(barrier, inc=1, device_id=peer, device_id_type=MESH)
 
@@ -293,7 +293,7 @@
     weight_part = jnp.dot(
         jnp.transpose(agg.astype(f32)).astype(bf16), slope, preferred_element_type=f32
     )
-    w_sem1, w_sem2, w_sem3, w_sem4, w_sem5, w_sem6 = (take(n) for n in (1, 3, 3, 3, 3, 1))
+    w_sem1, w_sem2, w_sem3, w_sem4, w_sem5, w_sem6 = (take(n) for n in (1, 3, 3, 3, 6, 1))
     for n in range(2):
         w1[n, 0:64] = weight_part[n * 64 : n * 64 + 64]
         w1[n, 64:72] = bias_part
@@ -399,7 +399,11 @@
     summed = in_order(z, w4[0], [w4[d] for d in (1, 2, 3)])
     scale = 1.0 / math.sqrt(256 * lax.axis_size("row") * lax.axis_size("col"))
     w5[core, y] = summed[0:16] * scale
-    w_got5 = [send(w5.at[core, y], w5.at[core, y], w_sem5 + d - 1, dy=d) for d in (1, 2, 3)]
+    mine = w5.at[core, y]
+    w_got5 = [send(mine, mine, w_sem6, dcore=1)]
+    for d in (1, 2, 3):
+        for other in range(2):
+            w_got5.append(send(mine, mine, w_sem5 + 2 * d - 2 + other, dy=d, dcore=other))
     bgrad_ref[...] = jnp.sum(summed[16:24], axis=0, keepdims=True) * scale
 
     got2 = []
@@ -414,15 +418,12 @@
             rs2_out[n] = total.astype(bf16)
             got2.append(send(rs2_out.at[n], rs2_in.at[n], rs_sem2 + n, dy=d))
 
-    for copy in w_got5:
-        copy.wait_recv()
-    w_got6 = send(w5.at[core], w5.at[core], w_sem6, dcore=1)
-
     for n in range(3):
         got2[n].wait_recv()
         total = total + rs2_in[n].astype(f32)
     fgrad_ref[...] = jnp.transpose(total)
-    w_got6.wait_recv()
+    for copy in w_got5:
+        copy.wait_recv()
     wgrad_ref[...] = w5[...].reshape(128, 256)
     for copy in sent:
         copy.wait_send()

time: 53 us -> 52 us (0.981)
  Pallas kernels: 51.6 us -> 50.6 us
    pallas_call x1, Pallas kernels: 50.8 us -> 49.8 us  [local(): pl.pallas_call(kernel, name='graph_layer', out_shape=(pltpu.VMEM((256, 25...]
where the time goes in v4:
time: 52 us; the launch traced here: 51.9 us
  Pallas kernels  50.6 us (97%)
  between operations  1.29 us (2%)
    pallas_call x1, Pallas kernels, local(): pl.pallas_call(kernel, name='graph_layer', out_shape=(pltpu.VMEM((256, 25...  49.8 us

profile of v4, /device:TPU:1, one launch (start us, length us, event | category | flops | bytes accessed | tf_op | source)
XLA Modules:
  0.0 51.9 jit_solution(1767764495290598319)
XLA Ops:
  1.3 49.8 %graph_layer.1 = (bf16[256,256]{1,0:T(8,128)(2,1)S(1)}, f32[128,256]{1,0:T(8,128)S(1)}, f32[1,256]{1,0:T(1,128)S(1)}, f32[256,128]{1,0:T(8,128)S(1)}) custom-call(bf16[256,128]{1,0:T(8,128)(2,1)} %feats_hbm.1, bf16[1,1,512,128,128]{4,3,2,1,0:T(8,128)(2,1)} %tiles_hbm.1, s32[1,1,2,512]{3,2,1,0:T(2,128)} %coords_hbm.1, s32[1,1]{1,0:T(1,128)S(6)} %copy.11.count_hbm, ...), custom_call_target="tpu_custom_call" | custom-call | tf_op jit(solution)/shard_map/graph_layer/pallas_call | solution.py:441
  51.1 0.8 %finish.1 = (bf16[256,256]{1,0:T(8,128)(2,1)}, f32[128,256]{1,0:T(8,128)}, f32[1,256]{1,0:T(1,128)}, f32[256,128]{1,0:T(8,128)}) custom-call(bf16[256,256]{1,0:T(8,128)(2,1)S(1)} %get-tuple-element.12.refs_0_, f32[128,256]{1,0:T(8,128)S(1)} %get-tuple-element.13.refs_1_, f32[1,256]{1,0:T(1,128)S(1)} %get-tuple-element.14.refs_2_, ...), custom_call_target="tpu_custom_call" | custom-call | tf_op jit(solution)/shard_map/finish/pallas_call | solution.py:492
